TPU v7x, 32 devices: a whole 2x2x4 slice. The times are simulated.
32 devices in a mesh: gx: 4 (over y, core), gy: 8 (over z, x).
Axes of the slice: x: 2, y: 2, z: 4, core: 2. Of those that a mesh axis runs over, the one named last changes fastest.
Arguments:
- tensor: float32 [1024, 1024, 8], P('gx', 'gy'), may hold values from -6 to 6
- sketch_one: float32 [1024, 8, 256], P('gy'), may hold values from -0.0625 to 0.0625
- sketch_two: float32 [256, 8, 256], P('gx'), may hold values from -0.125 to 0.125
Outputs:
- basis_one: float32 [1024, 256], P('gx')
- basis_two: float32 [1024, 256], P('gy')
- core: float32 [256, 256, 8], P('gx', 'gy')
All inputs are finite; a program needn't handle non-finite values.
Results may differ from a plain program's by a relative error of at most 0.00008.
Values sent between devices are 32-bit elements; how exact they have to be, the bound alone decides.
A program may use at most 64 MiB of HBM per device.

v0:
```python
import jax
import jax.numpy as jnp
from jax import lax
from jax.sharding import PartitionSpec as P


def gram_local(matrix):
    return jnp.dot(matrix.T, matrix, precision=lax.Precision.HIGHEST)


def apply_factor(gram_total, matrix):
    factor = jnp.linalg.cholesky(gram_total)
    return lax.linalg.triangular_solve(
        factor, matrix, left_side=False, lower=True, transpose_a=True
    )


def local(tensor, sketch_one, sketch_two):
    rows_one, rows_two, depth = tensor.shape
    width = sketch_one.shape[2]
    unfolded = tensor.reshape(rows_one, rows_two * depth)
    partial_sketch = jnp.dot(
        unfolded, sketch_one.reshape(rows_two * depth, width), precision=lax.Precision.HIGHEST
    )
    first_sketch = lax.psum(partial_sketch, "gy")
    gram_total = lax.psum(gram_local(first_sketch), "gx")
    basis_one = apply_factor(gram_total, first_sketch)
    rank_rows = width // lax.axis_size("gx")
    partial_core = lax.psum_scatter(
        lax.dot_general(
            basis_one, unfolded, (((0,), (0,)), ((), ())), precision=lax.Precision.HIGHEST
        ),
        "gx",
        scatter_dimension=0,
        tiled=True,
    )
    partial_core = partial_core.reshape(rank_rows, rows_two, depth)
    second_part = jnp.einsum(
        "rjk,rkc->jc", partial_core, sketch_two, precision=lax.Precision.HIGHEST
    )
    second_sketch = lax.psum(second_part, "gx")
    gram_second = lax.psum(gram_local(second_sketch), "gy")
    basis_two = apply_factor(gram_second, second_sketch)
    core_terms = jnp.einsum("rjk,js->rsk", partial_core, basis_two, precision=lax.Precision.HIGHEST)
    core = lax.psum_scatter(core_terms, "gy", scatter_dimension=1, tiled=True)
    return (basis_one, basis_two, core)


def solution(mesh):
    in_specs = (P("gx", "gy", None), P("gy", None, None), P("gx", None, None))
    out_specs = (P("gx", None), P("gy", None), P("gx", "gy", None))
    return jax.shard_map(local, mesh=mesh, in_specs=in_specs, out_specs=out_specs, check_vma=False)
```

profile of v0, /device:TPU:0, one launch (start us, length us, event | category | flops | bytes accessed | tf_op | source)
XLA Modules:
  0.0 453.2 jit_solution(10297458780907899300)
XLA Ops:
  7.2 1.8 copy.34
  9.1 2.5 convolution_bitcast_fusion.1
  11.7 73.6 %all-reduce.6.cloned.1.call-done = f32[256,256]{1,0:T(8,128)} async-done(((f32[256,256]{1,0:T(8,128)}), f32[256,256]{1,0:T(8,128)}) %all-reduce.6.cloned.1.call-update) | async-done | bytes 262160 | tf_op jit(solution)/shard_map/psum | solution.py:25
  85.2 2.3 fusion.22
  87.8 31.7 %all-reduce.8.cloned.1.call-done = f32[256,256]{0,1:T(8,128)} async-done(((f32[256,256]{0,1:T(8,128)}), f32[256,256]{0,1:T(8,128)}) %all-reduce.8.cloned.1.call-update) | async-done | bytes 262160 | tf_op jit(solution)/shard_map/psum | solution.py:26
  119.5 1.1 copy.36
  120.8 11.7 %cholesky.130 = f32[128,128]{1,0:T(8,128)S(1)} custom-call(f32[128,128]{1,0:T(8,128)S(1)} %cholesky.194), custom_call_target="Cholesky" | custom-call | tf_op jit(solution)/shard_map/jit(cholesky)/cholesky | solution.py:12
  132.5 9.8 %custom-call.17 = f32[1,128,128]{1,2,0:T(8,128)S(1)} custom-call(f32[1,128,128]{2,1,0:T(8,128)S(1)} %get-tuple-element.56), custom_call_target="InvertDiagBlocksLowerTriangular" | custom-call | tf_op jit(solution)/shard_map/jit(cholesky)/cholesky | solution.py:12
  142.8 11.7 %cholesky.147 = f32[128,128]{1,0:T(8,128)S(1)} custom-call(f32[128,128]{1,0:T(8,128)S(1)} %convolution_subtract_fusion.3), custom_call_target="Cholesky" | custom-call | tf_op jit(solution)/shard_map/jit(cholesky)/cholesky | solution.py:12
  156.7 4.2 while.2
  157.5 1.4 bitcast_dynamic-update-slice_fusion.4
  159.5 1.4 bitcast_dynamic-update-slice_fusion.4
  160.9 19.7 %custom-call.14 = f32[2,128,128]{1,2,0:T(8,128)S(1)} custom-call(f32[2,128,128]{2,1,0:T(8,128)S(1)} %get-tuple-element.11), custom_call_target="InvertDiagBlocksLowerTriangular" | custom-call | tf_op jit(solution)/shard_map/triangular_solve | solution.py:13
  181.6 2.0 fusion
  183.7 25.0 %reduce-scatter.3.cloned.1.call-done = f32[64,1024]{1,0:T(8,128)} async-done(((f32[256,1024]{1,0:T(8,128)}), f32[64,1024]{1,0:T(8,128)}) %reduce-scatter.3.cloned.1.call-update) | async-done | bytes 262160 | tf_op jit(solution)/shard_map/reduce_scatter | solution.py:29
  208.7 1.1 copy.38
  210.9 1.3 convolution_bitcast_fusion.2
  212.3 31.5 %all-reduce.10.cloned.1.call-done = f32[128,256]{1,0:T(8,128)} async-done(((f32[128,256]{1,0:T(8,128)}), f32[128,256]{1,0:T(8,128)}) %all-reduce.10.cloned.1.call-update) | async-done | bytes 131088 | tf_op jit(solution)/shard_map/psum | solution.py:41
  243.8 2.1 fusion.23
  246.0 72.2 %all-reduce.12.cloned.1.call-done = f32[256,256]{0,1:T(8,128)} async-done(((f32[256,256]{0,1:T(8,128)}), f32[256,256]{0,1:T(8,128)}) %all-reduce.12.cloned.1.call-update) | async-done | bytes 262160 | tf_op jit(solution)/shard_map/psum | solution.py:42
  318.2 1.1 copy.41
  319.4 11.7 %cholesky.164 = f32[128,128]{1,0:T(8,128)S(1)} custom-call(f32[128,128]{1,0:T(8,128)S(1)} %cholesky.197), custom_call_target="Cholesky" | custom-call | tf_op jit(solution)/shard_map/jit(cholesky)/cholesky | solution.py:12
  331.2 9.8 %custom-call.18 = f32[1,128,128]{1,2,0:T(8,128)S(1)} custom-call(f32[1,128,128]{2,1,0:T(8,128)S(1)} %get-tuple-element.52), custom_call_target="InvertDiagBlocksLowerTriangular" | custom-call | tf_op jit(solution)/shard_map/jit(cholesky)/cholesky | solution.py:12
  341.5 11.7 %cholesky.181 = f32[128,128]{1,0:T(8,128)S(1)} custom-call(f32[128,128]{1,0:T(8,128)S(1)} %convolution_subtract_fusion.2), custom_call_target="Cholesky" | custom-call | tf_op jit(solution)/shard_map/jit(cholesky)/cholesky | solution.py:12
  355.9 4.3 while.3
  356.7 1.4 bitcast_dynamic-update-slice_fusion.5
  358.7 1.4 bitcast_dynamic-update-slice_fusion.5
  360.1 19.7 %custom-call.15 = f32[2,128,128]{1,2,0:T(8,128)S(1)} custom-call(f32[2,128,128]{2,1,0:T(8,128)S(1)} %get-tuple-element.19), custom_call_target="InvertDiagBlocksLowerTriangular" | custom-call | tf_op jit(solution)/shard_map/triangular_solve | solution.py:13
  380.7 1.0 convolution_bitcast_fusion
  381.8 1.3 copy.44
  383.2 0.8 copy.45
  384.8 61.6 %reduce-scatter.5.cloned.1.call-done = f32[64,32,8]{0,2,1:T(8,128)} async-done(((f32[64,256,8]{0,2,1:T(8,128)}), f32[64,32,8]{0,2,1:T(8,128)}) %reduce-scatter.5.cloned.1.call-update) | async-done | bytes 65552 | tf_op jit(solution)/shard_map/reduce_scatter | solution.py:45
  (65 shorter events, 9.9 us)
Async XLA Ops:
  7.2 1.9 copy-start
  7.2 78.1 %all-reduce.6.cloned.1.call-start = ((), (), s32[]{:S(2)}) async-start(), calls=%async_computation.2 | async-start | bytes 524288 | tf_op jit(solution)/shard_map/psum | solution.py:25
  11.6 107.9 %all-reduce.8.cloned.1.call-start = ((), (), s32[]{:S(2)}) async-start(), calls=%async_computation.3 | async-start | bytes 524288 | tf_op jit(solution)/shard_map/psum | solution.py:26
  87.6 121.1 %reduce-scatter.3.cloned.1.call-start = ((), (), s32[]{:S(2)}) async-start(), calls=%async_computation.4 | async-start | bytes 1310720 | tf_op jit(solution)/shard_map/reduce_scatter | solution.py:29
  119.5 1.2 copy-start.3
  156.7 23.9 %copy-start.1 = (f32[256,256]{1,0:T(8,128)S(1)}, f32[256,256]{1,0:T(8,128)}, u32[]{:S(2)}) copy-start(f32[256,256]{1,0:T(8,128)} %all-reduce.6.cloned.1.call-done) | copy-start | bytes 786436
  183.7 60.1 %all-reduce.10.cloned.1.call-start = ((), (), s32[]{:S(2)}) async-start(), calls=%async_computation.5 | async-start | bytes 262144 | tf_op jit(solution)/shard_map/psum | solution.py:41
  209.9 1.0 copy-start.5
  212.2 106.0 %all-reduce.12.cloned.1.call-start = ((), (), s32[]{:S(2)}) async-start(), calls=%async_computation.6 | async-start | bytes 524288 | tf_op jit(solution)/shard_map/psum | solution.py:42
  245.9 200.5 %reduce-scatter.5.cloned.1.call-start = ((), (), s32[]{:S(2)}) async-start(), calls=%async_computation.7 | async-start | bytes 1179648 | tf_op jit(solution)/shard_map/reduce_scatter | solution.py:45
  318.2 1.2 copy-start.4
  355.8 24.0 %copy-start.2 = (f32[128,256]{1,0:T(8,128)S(1)}, f32[128,256]{1,0:T(8,128)}, u32[]{:S(2)}) copy-start(f32[128,256]{1,0:T(8,128)} %all-reduce.10.cloned.1.call-done) | copy-start | bytes 393220
Sparse Core Ops, SparseCore 0:
  11.9 73.2 all-reduce.5
  88.2 31.2 all-reduce.7
  183.8 24.8 reduce-scatter.2
  212.3 31.4 all-reduce.9
  247.6 70.5 all-reduce.11
  383.2 63.0 reduce-scatter.4
where the time goes:
time: 454 us; the launch traced here: 453 us
  waiting for transfers between devices  296 us (65%)
  other arithmetic  108 us (24%)
  local copies, waits for them, and re-layouts  17.2 us (4%)
  between operations  17 us (4%)
  matrix products  14.1 us (3%)
    psum x1, waiting for transfers between devices, local(): first_sketch = lax.psum(partial_sketch, 'gy')  73.6 us
    psum x1, waiting for transfers between devices, local(): gram_second = lax.psum(gram_local(second_sketch), 'gy')  72.2 us
    another operation x13, other arithmetic, apply_factor(): factor = jnp.linalg.cholesky(gram_total)  68.6 us
    reduce_scatter x1, waiting for transfers between devices, local(): core = lax.psum_scatter(core_terms, 'gy', scatter_dimension=1, tiled=True)  61.6 us
    another operation x7, other arithmetic, apply_factor(): lax.linalg.triangular_solve(factor, matrix, left_side=False, lower=True,...  39.4 us
    psum x1, waiting for transfers between devices, local(): gram_total = lax.psum(gram_local(first_sketch), 'gx')  31.7 us
    psum x1, waiting for transfers between devices, local(): second_sketch = lax.psum(second_part, 'gx')  31.5 us
    reduce_scatter x1, waiting for transfers between devices, local(): lax.psum_scatter(lax.dot_general(basis_one, unfolded, (((0,), (0,)), ((),...  25 us
  transfers between devices with their start and end apart: 6, of which 6 were waited for; matrix products, arithmetic and copies ran while one was open for 0% of the time, Pallas kernels for 0%

commit v1 on v0

v1 whole, which is shorter than its diff:
```python
import functools

import jax
import jax.numpy as jnp
from jax import lax
from jax.experimental import pallas as pl
from jax.experimental.pallas import tpu as pltpu
from jax.sharding import PartitionSpec as P

HIGHEST = lax.Precision.HIGHEST
MESH = pl.DeviceIdType.MESH
BLOCK = 64
VMEM_BYTES = 40 * 1024 * 1024


def gram_local(matrix):
    return jnp.dot(matrix.T, matrix, precision=HIGHEST)


def apply_factor(gram_total, matrix):
    factor = jnp.linalg.cholesky(gram_total)
    return lax.linalg.triangular_solve(
        factor, matrix, left_side=False, lower=True, transpose_a=True
    )


def local_plain(tensor, sketch_one, sketch_two):
    rows_one, rows_two, depth = tensor.shape
    width = sketch_one.shape[2]
    unfolded = tensor.reshape(rows_one, rows_two * depth)
    partial_sketch = jnp.dot(
        unfolded, sketch_one.reshape(rows_two * depth, width), precision=HIGHEST
    )
    first_sketch = lax.psum(partial_sketch, "gy")
    gram_total = lax.psum(gram_local(first_sketch), "gx")
    basis_one = apply_factor(gram_total, first_sketch)
    rank_rows = width // lax.axis_size("gx")
    partial_core = lax.psum_scatter(
        lax.dot_general(basis_one, unfolded, (((0,), (0,)), ((), ())), precision=HIGHEST),
        "gx",
        scatter_dimension=0,
        tiled=True,
    )
    partial_core = partial_core.reshape(rank_rows, rows_two, depth)
    second_part = jnp.einsum("rjk,rkc->jc", partial_core, sketch_two, precision=HIGHEST)
    second_sketch = lax.psum(second_part, "gx")
    gram_second = lax.psum(gram_local(second_sketch), "gy")
    basis_two = apply_factor(gram_second, second_sketch)
    core_terms = jnp.einsum("rjk,js->rsk", partial_core, basis_two, precision=HIGHEST)
    core = lax.psum_scatter(core_terms, "gy", scatter_dimension=1, tiled=True)
    return (basis_one, basis_two, core)


def nn(a, b):
    return jnp.dot(a, b, precision=HIGHEST, preferred_element_type=jnp.float32)


def nt(a, b):
    return lax.dot_general(
        a, b, (((1,), (1,)), ((), ())), precision=HIGHEST, preferred_element_type=jnp.float32
    )


def tn(a, b):
    return lax.dot_general(
        a, b, (((0,), (0,)), ((), ())), precision=HIGHEST, preferred_element_type=jnp.float32
    )


def eliminate(square):
    b = square.shape[0]
    eye = (
        lax.broadcasted_iota(jnp.int32, (b, b), 0) == lax.broadcasted_iota(jnp.int32, (b, b), 1)
    ).astype(jnp.float32)
    full = jnp.concatenate([square, eye], axis=1)
    lanes = 2 * b
    groups = [full[g * 8 : g * 8 + 8] for g in range(b // 8)]
    sub = lax.broadcasted_iota(jnp.int32, (8, lanes), 0)
    for g in range(b // 8):
        later = range(g, b // 8)
        cols = []
        for j in range(8):
            lane = g * 8 + j
            cols.append(
                {h: jnp.broadcast_to(groups[h][:, lane : lane + 1], (8, lanes)) for h in later}
            )
        panel = groups[g]
        scale = jnp.zeros((8, lanes), jnp.float32)
        scaled_rows = []
        for j in range(8):
            col = cols[j]
            head = col[g]
            pivot = jnp.broadcast_to(head[j : j + 1], (8, lanes))
            inverse = 1.0 / pivot
            scale = jnp.where(sub == j, pivot, scale)
            below = jnp.where(sub > j, head, 0.0)
            row = jnp.broadcast_to(panel[j : j + 1], (8, lanes)) * inverse
            scaled_rows.append(row)
            for l in range(j + 1, 8):
                factor = jnp.broadcast_to(head[l : l + 1], (8, lanes)) * inverse
                for h in later:
                    cols[l][h] = cols[l][h] - (below if h == g else col[h]) * factor
            panel = panel - below * row
        for h in later:
            if h > g:
                value = groups[h]
                for j in range(8):
                    value = value - cols[j][h] * scaled_rows[j]
                groups[h] = value
        groups[g] = panel * lax.rsqrt(scale)
    return jnp.concatenate(groups, axis=0)[:, b:]


def factor_inverse(gram, work):
    n = gram.shape[0]
    work[:, :n] = gram
    work[:, n:] = (
        lax.broadcasted_iota(jnp.int32, (n, n), 0) == lax.broadcasted_iota(jnp.int32, (n, n), 1)
    ).astype(jnp.float32)
    for start in range(0, n, BLOCK):
        stop = start + BLOCK
        inv = eliminate(work[start:stop, start:stop])
        rows = nn(inv, work[start:stop, :])
        if stop < n:
            panel = nt(work[stop:n, start:stop], inv)
            work[stop:n, :] = work[stop:n, :] - nn(panel, rows)
        work[start:stop, n:] = rows[:, n:]


def start_copy(source, target, send_sem, recv_sem, axis, peer):
    copy = pltpu.make_async_remote_copy(
        src_ref=source,
        dst_ref=target,
        send_sem=send_sem,
        recv_sem=recv_sem,
        device_id={axis: peer},
        device_id_type=MESH,
    )
    copy.start()
    return copy


def scatter_start(source, slots, send, recv, axis, size, chunk):
    me = lax.axis_index(axis)
    copies = []
    for d in range(1, size):
        peer = lax.rem(me + d, size)
        copies.append(
            start_copy(
                chunk(source, peer), slots.at[d - 1], send.at[d - 1], recv.at[d - 1], axis, peer
            )
        )
    return copies


def gather_start(target, send, recv, axis, size, chunk):
    me = lax.axis_index(axis)
    copies = []
    for d in range(1, size):
        peer = lax.rem(me + d, size)
        mine = chunk(target, me)
        copies.append(start_copy(mine, mine, send.at[d - 1], recv.at[d - 1], axis, peer))
    return copies


def finish(copies):
    for copy in copies:
        copy.wait()


def row_chunk(rows):
    def chunk(ref, index):
        return ref.at[pl.ds(pl.multiple_of(index * rows, rows), rows)]

    return chunk


def lead_chunk(ref, index):
    return ref.at[index]


def all_reduce(ref, out, slots, send, recv, axis, size):
    me = lax.axis_index(axis)
    rows = ref.shape[0] // size
    chunk = row_chunk(rows)
    finish(scatter_start(ref, slots, send.at[0], recv.at[0], axis, size, chunk))
    mine = pl.ds(pl.multiple_of(me * rows, rows), rows)
    total = ref[mine, :]
    for d in range(size - 1):
        total = total + slots[d]
    out[mine, :] = total
    finish(gather_start(out, send.at[1], recv.at[1], axis, size, chunk))


def barrier_all(gx, gy):
    barrier = pltpu.get_barrier_semaphore()
    for axis, size in (("gx", gx), ("gy", gy)):
        me = lax.axis_index(axis)
        for d in range(1, size):
            pl.semaphore_signal(
                barrier, inc=1, device_id={axis: lax.rem(me + d, size)}, device_id_type=MESH
            )
    pl.semaphore_wait(barrier, gx + gy - 2)


def first_kernel(
    gx, gy, t_ref, s1_ref, s2_ref, y_ref, gram_ref, z_ref, s2_out,
    ypart, yfull, gpart, gfull, zall, s2_all, s2_got, yslots, gslots, zslots,
    ysend, yrecv, gsend, grecv, zsend, zrecv, ssend, srecv,
):
    depth = t_ref.shape[1]
    mine = lax.axis_index("gx")
    per = depth // gx
    for k in range(depth):
        s2_all[k // per, k % per] = s2_ref[:, k, :]
    barrier_all(gx, gy)
    moving = scatter_start(s2_all, s2_got, ssend, srecv, "gx", gx, lead_chunk)
    total = nn(t_ref[:, 0, :], s1_ref[:, 0, :])
    for k in range(1, depth):
        total = total + nn(t_ref[:, k, :], s1_ref[:, k, :])
    ypart[...] = total
    all_reduce(ypart, yfull, yslots, ysend, yrecv, "gy", gy)
    y = yfull[...]
    y_ref[...] = y
    yt = y.T
    gpart[...] = nn(yt, y)
    for k in range(depth):
        zall[k // per, k % per] = nn(yt, t_ref[:, k, :])
    zmove = scatter_start(zall, zslots, zsend, zrecv, "gx", gx, lead_chunk)
    all_reduce(gpart, gfull, gslots, gsend, grecv, "gx", gx)
    gram_ref[...] = gfull[...]
    finish(zmove)
    z = zall[mine]
    for d in range(gx - 1):
        z = z + zslots[d]
    z_ref[...] = z
    finish(moving)
    s2_out[mine] = s2_all[mine]
    for d in range(1, gx):
        s2_out[lax.rem(mine + gx - d, gx)] = s2_got[d - 1]


def second_kernel(y_ref, gram_ref, z_ref, q_ref, p_ref, work):
    n = gram_ref.shape[0]
    factor_inverse(gram_ref[...], work)
    inv = work[:, n:]
    q_ref[...] = nt(y_ref[...], inv)
    for k in range(z_ref.shape[0]):
        p_ref[k] = nn(inv, z_ref[k])


def third_kernel(
    gx, gy, p_ref, s2_ref, sketch_ref, gram_ref, w_ref,
    spart, sfull, gpart, gfull, wall, sslots, gslots, wslots,
    ssend, srecv, gsend, grecv, wsend, wrecv,
):
    per = p_ref.shape[0]
    barrier_all(gx, gy)
    rows = s2_ref.shape[2]
    total = None
    for k in range(per):
        for a in range(gx):
            term = tn(p_ref[k, a * rows : (a + 1) * rows, :], s2_ref[a, k])
            total = term if total is None else total + term
    spart[...] = total
    all_reduce(spart, sfull, sslots, ssend, srecv, "gx", gx)
    sketch = sfull[...]
    sketch_ref[...] = sketch
    gpart[...] = tn(sketch, sketch)
    part = wall.shape[2]
    for k in range(per):
        w = nn(p_ref[k], sketch)
        for g in range(gy):
            wall[g, k] = w[g * part : (g + 1) * part]
    wmove = scatter_start(wall, wslots, wsend, wrecv, "gy", gy, lead_chunk)
    all_reduce(gpart, gfull, gslots, gsend, grecv, "gy", gy)
    gram_ref[...] = gfull[...]
    finish(wmove)
    value = wall[lax.axis_index("gy")]
    for d in range(gy - 1):
        value = value + wslots[d]
    w_ref[...] = value


def fourth_kernel(sketch_ref, gram_ref, w_ref, q_ref, out_ref, work):
    n = gram_ref.shape[0]
    factor_inverse(gram_ref[...], work)
    q_ref[...] = nt(sketch_ref[...], work[:, n:])
    pieces, _, _, width = out_ref.shape
    for g in range(pieces):
        inv = work[g * width : (g + 1) * width, n:]
        for k in range(w_ref.shape[0]):
            out_ref[g, k] = nt(w_ref[k], inv)


def fifth_kernel(gx, gy, piece_ref, out_ref, got, send, recv):
    a, b = lax.axis_index("gx"), lax.axis_index("gy")
    ratio = gy // gx
    barrier = pltpu.get_barrier_semaphore()
    inside = b // ratio == a
    for sa in range(gx):
        for sb in range(ratio):
            @pl.when(jnp.logical_not(jnp.logical_and(sa == a, a * ratio + sb == b)))
            def _():
                pl.semaphore_signal(
                    barrier, inc=1, device_id={"gx": sa, "gy": a * ratio + sb}, device_id_type=MESH
                )
    pl.semaphore_wait(barrier, gy - jnp.where(inside, 1, 0))
    slot = a * ratio + lax.rem(b, ratio)

    def outgoing(g):
        return pltpu.make_async_remote_copy(
            src_ref=piece_ref.at[g],
            dst_ref=got.at[slot],
            send_sem=send.at[g],
            recv_sem=recv.at[slot],
            device_id={"gx": b // ratio, "gy": g},
            device_id_type=MESH,
        )

    for g in range(gy):
        own = jnp.logical_and(inside, g == b)

        @pl.when(jnp.logical_not(own))
        def _():
            outgoing(g).start()

    for g in range(gy):
        own = jnp.logical_and(inside, g == b)

        @pl.when(jnp.logical_not(own))
        def _():
            outgoing(g).wait_send()

    for s in range(gx * ratio):
        own = jnp.logical_and(inside, s == slot)

        @pl.when(jnp.logical_not(own))
        def _():
            pltpu.make_async_remote_copy(
                src_ref=piece_ref.at[0],
                dst_ref=got.at[s],
                send_sem=send.at[0],
                recv_sem=recv.at[s],
                device_id={"gx": b // ratio, "gy": 0},
                device_id_type=MESH,
            ).wait_recv()

            out_ref[s] = got[s]

        @pl.when(own)
        def _():
            out_ref[s] = piece_ref[b]


def call(body, outs, scratch, collective_id, *args):
    vmem = pl.BlockSpec(memory_space=pltpu.VMEM)
    if collective_id is None:
        params = pltpu.CompilerParams(vmem_limit_bytes=VMEM_BYTES)
    else:
        params = pltpu.CompilerParams(
            vmem_limit_bytes=VMEM_BYTES, collective_id=collective_id, has_side_effects=True
        )
    return pl.pallas_call(
        body,
        out_shape=[jax.ShapeDtypeStruct(shape, jnp.float32) for shape in outs],
        in_specs=[vmem] * len(args),
        out_specs=[vmem] * len(outs),
        scratch_shapes=scratch,
        compiler_params=params,
    )(*args)


def local_kernels(gx, gy, tensor, sketch_one, sketch_two):
    rows_one, rows_two, depth = tensor.shape
    width = sketch_one.shape[2]
    ranks = sketch_two.shape[0]
    per = depth // gx
    part = width // gy
    f32 = jnp.float32
    V = lambda *shape: pltpu.VMEM(shape, f32)
    D = lambda *shape: pltpu.SemaphoreType.DMA(shape)
    turned = jnp.swapaxes(tensor, 1, 2)
    y, gram, z, s2 = call(
        functools.partial(first_kernel, gx, gy),
        [(rows_one, width), (width, width), (per, width, rows_two), (gx, per, ranks, width)],
        [
            V(rows_one, width), V(rows_one, width), V(width, width), V(width, width),
            V(gx, per, width, rows_two),
            V(gx, per, ranks, width), V(gx - 1, per, ranks, width),
            V(gy - 1, rows_one // gy, width), V(gx - 1, width // gx, width),
            V(gx - 1, per, width, rows_two),
            D(2, gy - 1), D(2, gy - 1), D(2, gx - 1), D(2, gx - 1),
            D(gx - 1), D(gx - 1), D(gx - 1), D(gx - 1),
        ],
        1,
        turned, sketch_one, sketch_two,
    )
    basis_one, p = call(
        second_kernel,
        [(rows_one, width), (per, width, rows_two)],
        [V(width, 2 * width)],
        None,
        y, gram, z,
    )
    sketch, gram_second, w = call(
        functools.partial(third_kernel, gx, gy),
        [(rows_two, width), (width, width), (per, part, width)],
        [
            V(rows_two, width), V(rows_two, width), V(width, width), V(width, width),
            V(gy, per, part, width),
            V(gx - 1, rows_two // gx, width), V(gy - 1, width // gy, width),
            V(gy - 1, per, part, width),
            D(2, gx - 1), D(2, gx - 1), D(2, gy - 1), D(2, gy - 1), D(gy - 1), D(gy - 1),
        ],
        2,
        p, s2,
    )
    basis_two, pieces = call(
        fourth_kernel,
        [(rows_two, width), (gy, per, part, part)],
        [V(width, 2 * width)],
        None,
        sketch, gram_second, w,
    )
    (got,) = call(
        functools.partial(fifth_kernel, gx, gy),
        [(gy, per, part, part)],
        [V(gy, per, part, part), D(gy), D(gy)],
        3,
        pieces,
    )
    core = got.reshape(gx, gy // gx, per, part, part).transpose(1, 3, 4, 0, 2)
    core = core.reshape(ranks, part, depth)
    return basis_one, basis_two, core


def solution(mesh):
    gx, gy = mesh.shape["gx"], mesh.shape["gy"]

    def local(tensor, sketch_one, sketch_two):
        rows_one, rows_two, depth = tensor.shape
        width = sketch_one.shape[2]
        fits = (
            gx > 1
            and gy % gx == 0
            and depth % gx == 0
            and width % BLOCK == 0
            and rows_two % (8 * gx) == 0
            and rows_one % (8 * gy) == 0
            and width % (8 * gy) == 0
        )
        if fits:
            return local_kernels(gx, gy, tensor, sketch_one, sketch_two)
        return local_plain(tensor, sketch_one, sketch_two)

    in_specs = (P("gx", "gy", None), P("gy", None, None), P("gx", None, None))
    out_specs = (P("gx", None), P("gy", None), P("gx", "gy", None))
    return jax.shard_map(local, mesh=mesh, in_specs=in_specs, out_specs=out_specs, check_vma=False)
```

time: 454 us -> 121 us (0.27)
  waiting for transfers between devices: 296 us -> 0 us
  Pallas kernels: 0 us -> 114 us
  other arithmetic: 108 us -> 0 us
  between operations: 17 us -> 0.67 us
  matrix products: 14.1 us -> 0 us
  local copies, waits for them, and re-layouts: 17.2 us -> 4.56 us
    psum x4 -> x0, waiting for transfers between devices: 209 us -> none  [the longest x1 73.6 us: local(): first_sketch = lax.psum(partial_sketch, 'gy')]
    pallas_call x0 -> x5, Pallas kernels: none -> 114 us  [call(): pl.pallas_call(body, out_shape=[jax.ShapeDtypeStruct(shape, jnp.float32)...]
    another operation x20 -> x0, other arithmetic: 108 us -> none  [the longest x13 68.6 us: apply_factor(): factor = jnp.linalg.cholesky(gram_total)]
    reduce_scatter x2 -> x0, waiting for transfers between devices: 86.6 us -> none  [the longest x1 61.6 us: local(): core = lax.psum_scatter(core_terms, 'gy', scatter_dimension=1, tiled=True)]
    dot_general x6 -> x0, matrix products: 11.3 us -> none  [the longest x2 4.42 us: gram_local(): return jnp.dot(matrix.T, matrix, precision=lax.Precision.HIGHEST)]
    another operation x17 -> x0, local copies, waits for them, and re-layouts: 7.97 us -> none
  transfers between devices with their start and end apart: 6 -> 0, of which waited for: 6 -> 0; matrix products, arithmetic and copies ran while one was open for 0% -> 0% of each run, Pallas kernels for 0% -> 0%
where the time goes in v1:
time: 121 us; the launch traced here: 119 us
  Pallas kernels  114 us (94%)
  local copies, waits for them, and re-layouts  4.56 us (4%)
    pallas_call x5, Pallas kernels, call(): pl.pallas_call(body, out_shape=[jax.ShapeDtypeStruct(shape, jnp.float32)...  114 us
    unnamed x6, local copies, waits for them, and re-layouts  3.48 us

profile of v1, /device:TPU:0, one launch (start us, length us, event | category | flops | bytes accessed | tf_op | source)
XLA Modules:
  0.0 119.4 jit_solution(4729988431325486379)
XLA Ops:
  0.6 0.0 copy-start
  0.6 1.2 %copy-done = f32[256,128,8]{1,2,0:T(8,128)S(1)} copy-done((f32[256,128,8]{1,2,0:T(8,128)S(1)}, f32[256,128,8]{1,2,0:T(8,128)}, u32[]{:S(2)}) %copy-start) | copy-done | bytes 1048600
  1.9 0.0 copy-start.1
  1.9 1.2 %copy-done.1 = f32[128,8,256]{2,1,0:T(8,128)S(1)} copy-done((f32[128,8,256]{2,1,0:T(8,128)S(1)}, f32[128,8,256]{2,1,0:T(8,128)}, u32[]{:S(2)}) %copy-start.1) | copy-done | bytes 1048600
  3.1 0.0 copy-start.2
  3.1 1.0 copy-done.2
  4.1 43.4 %shard_map.58 = (f32[256,256]{1,0:T(8,128)S(1)}, f32[256,256]{1,0:T(8,128)S(1)}, f32[2,256,128]{2,1,0:T(8,128)S(1)}, f32[4,2,64,256]{3,2,1,0:T(8,128)S(1)}) custom-call(f32[256,8,128]{2,1,0:T(8,128)S(1)} %bitcast.6, f32[128,8,256]{2,1,0:T(8,128)S(1)} %copy-done.1, f32[64,8,256]{2,1,0:T(8,128)S(1)} %copy-done.2), custom_call_target="tpu_custom_call" | custom-call | tf_op jit(solution)/shard_map/pallas_call | solution.py:364
  47.5 11.1 %shard_map.59 = (f32[256,256]{1,0:T(8,128)}, f32[2,256,128]{2,1,0:T(8,128)S(1)}) custom-call(f32[256,256]{1,0:T(8,128)S(1)} %get-tuple-element.14.y_ref, f32[256,256]{1,0:T(8,128)S(1)} %get-tuple-element.15.gram_ref, f32[2,256,128]{2,1,0:T(8,128)S(1)} %get-tuple-element.16.z_ref), custom_call_target="tpu_custom_call" | custom-call | tf_op jit(solution)/shard_map/pallas_call | solution.py:364
  58.7 39.6 %shard_map.60 = (f32[128,256]{1,0:T(8,128)S(1)}, f32[256,256]{1,0:T(8,128)S(1)}, f32[2,32,256]{2,1,0:T(8,128)S(1)}) custom-call(f32[2,256,128]{2,1,0:T(8,128)S(1)} %get-tuple-element.18.p_ref, f32[4,2,64,256]{3,2,1,0:T(8,128)S(1)} %get-tuple-element.19.s2_ref), custom_call_target="tpu_custom_call" | custom-call | tf_op jit(solution)/shard_map/pallas_call | solution.py:364
  98.3 10.9 %shard_map.61 = (f32[128,256]{1,0:T(8,128)}, f32[8,2,32,32]{3,2,1,0:T(8,128)S(1)}) custom-call(f32[128,256]{1,0:T(8,128)S(1)} %get-tuple-element.20.sketch_ref, f32[256,256]{1,0:T(8,128)S(1)} %get-tuple-element.21.gram_ref, f32[2,32,256]{2,1,0:T(8,128)S(1)} %get-tuple-element.22.w_ref), custom_call_target="tpu_custom_call" | custom-call | tf_op jit(solution)/shard_map/pallas_call | solution.py:364
  109.2 9.1 %shard_map.62 = f32[8,2,32,32]{3,2,1,0:T(8,128)S(1)} custom-call(f32[8,2,32,32]{3,2,1,0:T(8,128)S(1)} %get-tuple-element.24.piece_ref), custom_call_target="tpu_custom_call" | custom-call | tf_op jit(solution)/shard_map/pallas_call | solution.py:364
  118.3 0.2 copy.6
  118.5 0.8 reshape.13
Async XLA Ops:
  0.6 1.2 %copy-start = (f32[256,128,8]{1,2,0:T(8,128)S(1)}, f32[256,128,8]{1,2,0:T(8,128)}, u32[]{:S(2)}) copy-start(f32[256,128,8]{1,2,0:T(8,128)} %param.3) | copy-start | bytes 3145732
  1.9 1.2 %copy-start.1 = (f32[128,8,256]{2,1,0:T(8,128)S(1)}, f32[128,8,256]{2,1,0:T(8,128)}, u32[]{:S(2)}) copy-start(f32[128,8,256]{2,1,0:T(8,128)} %s1_ref.1) | copy-start | bytes 3145732
  3.1 1.0 copy-start.2

commit v2 on v1

v2 whole, which is shorter than its diff:
```python
import functools

import jax
import jax.numpy as jnp
from jax import lax
from jax.experimental import pallas as pl
from jax.experimental.pallas import tpu as pltpu
from jax.sharding import PartitionSpec as P

HIGHEST = lax.Precision.HIGHEST
MESH = pl.DeviceIdType.MESH
BLOCK = 64
VMEM_BYTES = 56 * 1024 * 1024


def gram_local(matrix):
    return jnp.dot(matrix.T, matrix, precision=HIGHEST)


def apply_factor(gram_total, matrix):
    factor = jnp.linalg.cholesky(gram_total)
    return lax.linalg.triangular_solve(
        factor, matrix, left_side=False, lower=True, transpose_a=True
    )


def local_plain(tensor, sketch_one, sketch_two):
    rows_one, rows_two, depth = tensor.shape
    width = sketch_one.shape[2]
    unfolded = tensor.reshape(rows_one, rows_two * depth)
    partial_sketch = jnp.dot(
        unfolded, sketch_one.reshape(rows_two * depth, width), precision=HIGHEST
    )
    first_sketch = lax.psum(partial_sketch, "gy")
    gram_total = lax.psum(gram_local(first_sketch), "gx")
    basis_one = apply_factor(gram_total, first_sketch)
    rank_rows = width // lax.axis_size("gx")
    partial_core = lax.psum_scatter(
        lax.dot_general(basis_one, unfolded, (((0,), (0,)), ((), ())), precision=HIGHEST),
        "gx",
        scatter_dimension=0,
        tiled=True,
    )
    partial_core = partial_core.reshape(rank_rows, rows_two, depth)
    second_part = jnp.einsum("rjk,rkc->jc", partial_core, sketch_two, precision=HIGHEST)
    second_sketch = lax.psum(second_part, "gx")
    gram_second = lax.psum(gram_local(second_sketch), "gy")
    basis_two = apply_factor(gram_second, second_sketch)
    core_terms = jnp.einsum("rjk,js->rsk", partial_core, basis_two, precision=HIGHEST)
    core = lax.psum_scatter(core_terms, "gy", scatter_dimension=1, tiled=True)
    return (basis_one, basis_two, core)


def nn(a, b):
    return jnp.dot(a, b, precision=HIGHEST, preferred_element_type=jnp.float32)


def nt(a, b):
    return lax.dot_general(
        a, b, (((1,), (1,)), ((), ())), precision=HIGHEST, preferred_element_type=jnp.float32
    )


def tn(a, b):
    return lax.dot_general(
        a, b, (((0,), (0,)), ((), ())), precision=HIGHEST, preferred_element_type=jnp.float32
    )


def eliminate(square):
    b = square.shape[0]
    eye = (
        lax.broadcasted_iota(jnp.int32, (b, b), 0) == lax.broadcasted_iota(jnp.int32, (b, b), 1)
    ).astype(jnp.float32)
    full = jnp.concatenate([square, eye], axis=1)
    lanes = 2 * b
    groups = [full[g * 8 : g * 8 + 8] for g in range(b // 8)]
    sub = lax.broadcasted_iota(jnp.int32, (8, lanes), 0)
    for g in range(b // 8):
        later = range(g, b // 8)
        cols = []
        for j in range(8):
            lane = g * 8 + j
            cols.append(
                {h: jnp.broadcast_to(groups[h][:, lane : lane + 1], (8, lanes)) for h in later}
            )
        panel = groups[g]
        scale = jnp.zeros((8, lanes), jnp.float32)
        scaled_rows = []
        for j in range(8):
            col = cols[j]
            head = col[g]
            pivot = jnp.broadcast_to(head[j : j + 1], (8, lanes))
            inverse = 1.0 / pivot
            scale = jnp.where(sub == j, pivot, scale)
            below = jnp.where(sub > j, head, 0.0)
            row = jnp.broadcast_to(panel[j : j + 1], (8, lanes)) * inverse
            scaled_rows.append(row)
            for l in range(j + 1, 8):
                factor = jnp.broadcast_to(head[l : l + 1], (8, lanes)) * inverse
                for h in later:
                    cols[l][h] = cols[l][h] - (below if h == g else col[h]) * factor
            panel = panel - below * row
        for h in later:
            if h > g:
                value = groups[h]
                for j in range(8):
                    value = value - cols[j][h] * scaled_rows[j]
                groups[h] = value
        groups[g] = panel * lax.rsqrt(scale)
    return jnp.concatenate(groups, axis=0)[:, b:]


def factor_inverse(gram, work):
    n = gram.shape[0]
    work[:, :n] = gram
    work[:, n : 2 * n] = (
        lax.broadcasted_iota(jnp.int32, (n, n), 0) == lax.broadcasted_iota(jnp.int32, (n, n), 1)
    ).astype(jnp.float32)
    for start in range(0, n, BLOCK):
        stop = start + BLOCK
        inv = eliminate(work[start:stop, start:stop])
        rows = nn(inv, work[start:stop, :])
        if stop < n:
            panel = nt(work[stop:n, start:stop], inv)
            work[stop:n, :] = work[stop:n, :] - nn(panel, rows)
        work[start:stop, n:] = rows[:, n:]


def start_copy(source, target, send_sem, recv_sem, axis, peer):
    copy = pltpu.make_async_remote_copy(
        src_ref=source,
        dst_ref=target,
        send_sem=send_sem,
        recv_sem=recv_sem,
        device_id={axis: peer},
        device_id_type=MESH,
    )
    copy.start()
    return copy


def scatter_start(source, slots, send, recv, axis, size, chunk):
    me = lax.axis_index(axis)
    copies = []
    for d in range(1, size):
        peer = lax.rem(me + d, size)
        copies.append(
            start_copy(
                chunk(source, peer), slots.at[d - 1], send.at[d - 1], recv.at[d - 1], axis, peer
            )
        )
    return copies


def gather_start(target, send, recv, axis, size, chunk):
    me = lax.axis_index(axis)
    copies = []
    for d in range(1, size):
        peer = lax.rem(me + d, size)
        mine = chunk(target, me)
        copies.append(start_copy(mine, mine, send.at[d - 1], recv.at[d - 1], axis, peer))
    return copies


def finish(copies):
    for copy in copies:
        copy.wait()


def row_chunk(rows):
    def chunk(ref, index):
        return ref.at[pl.ds(pl.multiple_of(index * rows, rows), rows)]

    return chunk


def lead_chunk(ref, index):
    return ref.at[index]


def barrier_all(gx, gy):
    a, b = lax.axis_index("gx"), lax.axis_index("gy")
    ratio = gy // gx
    barrier = pltpu.get_barrier_semaphore()
    for axis, size, me in (("gx", gx, a), ("gy", gy, b)):
        for d in range(1, size):
            pl.semaphore_signal(
                barrier, inc=1, device_id={axis: lax.rem(me + d, size)}, device_id_type=MESH
            )
    for sa in range(gx):
        for sb in range(ratio):
            @pl.when(jnp.logical_not(jnp.logical_and(sa == a, a * ratio + sb == b)))
            def _():
                pl.semaphore_signal(
                    barrier, inc=1, device_id={"gx": sa, "gy": a * ratio + sb}, device_id_type=MESH
                )
    pl.semaphore_wait(barrier, gx + gy - 2 + gy - jnp.where(b // ratio == a, 1, 0))


def sum_chunk(ref, slots, mine):
    total = ref[mine]
    for d in range(slots.shape[0]):
        total = total + slots[d]
    return total


def reduce_rows(part, out, slots, send, recv, axis, size, beside=None, after=None):
    me = lax.axis_index(axis)
    rows = part.shape[0] // size
    chunk = row_chunk(rows)
    copies = scatter_start(part, slots, send.at[0], recv.at[0], axis, size, chunk)
    if beside is not None:
        beside()
    finish(copies)
    mine = pl.ds(pl.multiple_of(me * rows, rows), rows)
    out[mine, :] = sum_chunk(part, slots, mine)
    copies = gather_start(out, send.at[1], recv.at[1], axis, size, chunk)
    if after is not None:
        after()
    finish(copies)


def exchange_pieces(gx, gy, pieces, got, out_ref, send, recv):
    a, b = lax.axis_index("gx"), lax.axis_index("gy")
    ratio = gy // gx
    inside = b // ratio == a
    slot = a * ratio + lax.rem(b, ratio)

    def outgoing(g):
        return pltpu.make_async_remote_copy(
            src_ref=pieces.at[g],
            dst_ref=got.at[slot],
            send_sem=send.at[g],
            recv_sem=recv.at[slot],
            device_id={"gx": b // ratio, "gy": g},
            device_id_type=MESH,
        )

    for g in range(gy):
        @pl.when(jnp.logical_not(jnp.logical_and(inside, g == b)))
        def _():
            outgoing(g).start()

    for s in range(gx * ratio):
        own = jnp.logical_and(inside, s == slot)

        @pl.when(jnp.logical_not(own))
        def _():
            pltpu.make_async_remote_copy(
                src_ref=pieces.at[0],
                dst_ref=got.at[s],
                send_sem=send.at[0],
                recv_sem=recv.at[s],
                device_id={"gx": b // ratio, "gy": 0},
                device_id_type=MESH,
            ).wait_recv()
            out_ref[s] = got[s]

        @pl.when(own)
        def _():
            out_ref[s] = pieces[b]

    for g in range(gy):
        @pl.when(jnp.logical_not(jnp.logical_and(inside, g == b)))
        def _():
            outgoing(g).wait_send()


def kernel(
    gx, gy, t_hbm, s1_hbm, s2_hbm, q1_ref, q2_ref, out_ref,
    t_ref, s1_ref, s2_ref, load, work,
    ypart, yfull, yslots, ysend, yrecv,
    gpart, gfull, gslots, gsend, grecv,
    zall, zslots, zsend, zrecv,
    s2_all, s2_got, s2send, s2recv,
    spart, sfull, sslots, ssend, srecv,
    hpart, hfull, hslots, hsend, hrecv,
    wall, wslots, wsend, wrecv,
    pieces, got, esend, erecv,
):
    depth = t_ref.shape[1]
    width = s1_ref.shape[2]
    a, b = lax.axis_index("gx"), lax.axis_index("gy")
    per = depth // gx
    loads = [
        pltpu.make_async_copy(src, dst, load.at[i])
        for i, (src, dst) in enumerate(((s1_hbm, s1_ref), (t_hbm, t_ref), (s2_hbm, s2_ref)))
    ]
    for copy in loads:
        copy.start()
    barrier_all(gx, gy)
    finish(loads)

    total = nn(t_ref[:, 0, :], s1_ref[:, 0, :])
    for k in range(1, depth):
        total = total + nn(t_ref[:, k, :], s1_ref[:, k, :])
    ypart[...] = total

    for_later = []

    def send_sketch():
        for k in range(depth):
            s2_all[k // per, k % per] = s2_ref[:, k, :]
        for_later.extend(scatter_start(s2_all, s2_got, s2send, s2recv, "gx", gx, lead_chunk))

    reduce_rows(ypart, yfull, yslots, ysend, yrecv, "gy", gy, beside=send_sketch)

    y = yfull[...]
    yt = y.T
    gpart[...] = nn(yt, y)
    z_moves = []

    def contract():
        for k in range(depth):
            zall[k // per, k % per] = nn(yt, t_ref[:, k, :])

    def send_contraction():
        z_moves.extend(scatter_start(zall, zslots, zsend, zrecv, "gx", gx, lead_chunk))

    reduce_rows(
        gpart, gfull, gslots, gsend, grecv, "gx", gx, beside=contract, after=send_contraction
    )
    factor_inverse(gfull[...], work)
    inv = work[:, width : 2 * width]
    q1_ref[...] = nt(yfull[...], inv)
    finish(z_moves)
    z = sum_chunk(zall, zslots, a)
    p = [nn(inv, z[k]) for k in range(per)]

    finish(for_later)
    ranks = s2_all.shape[2]
    s2_got_all = s2_all.at[a]
    total = None
    for d in range(gx):
        origin = lax.rem(a + gx - d, gx)
        for k in range(per):
            block = s2_got_all[k] if d == 0 else s2_got[d - 1, k]
            work[pl.ds(pl.multiple_of(origin * ranks, ranks), ranks), k * width : (k + 1) * width] = (
                block
            )
    for k in range(per):
        term = tn(p[k], work[:, k * width : (k + 1) * width])
        total = term if total is None else total + term
    spart[...] = total
    reduce_rows(spart, sfull, sslots, ssend, srecv, "gx", gx)

    sketch = sfull[...]
    hpart[...] = tn(sketch, sketch)
    part = wall.shape[2]
    w_moves = []

    def contract_second():
        for k in range(per):
            w = nn(p[k], sketch)
            for g in range(gy):
                wall[g, k] = w[g * part : (g + 1) * part]

    def send_second():
        w_moves.extend(scatter_start(wall, wslots, wsend, wrecv, "gy", gy, lead_chunk))

    reduce_rows(
        hpart, hfull, hslots, hsend, hrecv, "gy", gy, beside=contract_second, after=send_second
    )
    factor_inverse(hfull[...], work)
    q2_ref[...] = nt(sfull[...], work[:, width:])
    finish(w_moves)
    w = sum_chunk(wall, wslots, b)
    for g in range(gy):
        inv = work[g * part : (g + 1) * part, width:]
        for k in range(per):
            pieces[g, k] = nt(w[k], inv)
    exchange_pieces(gx, gy, pieces, got, out_ref, esend, erecv)


def local_kernels(gx, gy, tensor, sketch_one, sketch_two):
    rows_one, rows_two, depth = tensor.shape
    width = sketch_one.shape[2]
    per = depth // gx
    ranks = sketch_two.shape[0]
    part = width // gy
    f32 = jnp.float32
    V = lambda *shape: pltpu.VMEM(shape, f32)
    D = lambda *shape: pltpu.SemaphoreType.DMA(shape)

    def sums(rows, size):
        return [
            V(rows, width), V(rows, width), V(size - 1, rows // size, width),
            D(2, size - 1), D(2, size - 1),
        ]

    turned = jnp.swapaxes(tensor, 1, 2)
    vmem = pl.BlockSpec(memory_space=pltpu.VMEM)
    basis_one, basis_two, got = pl.pallas_call(
        functools.partial(kernel, gx, gy),
        out_shape=[
            jax.ShapeDtypeStruct((rows_one, width), f32),
            jax.ShapeDtypeStruct((rows_two, width), f32),
            jax.ShapeDtypeStruct((gy, per, part, part), f32),
        ],
        in_specs=[pl.BlockSpec(memory_space=pl.ANY)] * 3,
        out_specs=[vmem] * 3,
        scratch_shapes=[
            V(*turned.shape), V(*sketch_one.shape), V(*sketch_two.shape), D(3),
            V(width, max(2, per) * width),
            *sums(rows_one, gy),
            *sums(width, gx),
            V(gx, per, width, rows_two), V(gx - 1, per, width, rows_two), D(gx - 1), D(gx - 1),
            V(gx, per, ranks, width), V(gx - 1, per, ranks, width), D(gx - 1), D(gx - 1),
            *sums(rows_two, gx),
            *sums(width, gy),
            V(gy, per, part, width), V(gy - 1, per, part, width), D(gy - 1), D(gy - 1),
            V(gy, per, part, part), V(gy, per, part, part), D(gy), D(gy),
        ],
        compiler_params=pltpu.CompilerParams(
            vmem_limit_bytes=VMEM_BYTES, collective_id=1, has_side_effects=True
        ),
    )(turned, sketch_one, sketch_two)
    core = got.reshape(gx, gy // gx, per, part, part).transpose(1, 3, 4, 0, 2)
    return basis_one, basis_two, core.reshape(ranks, part, depth)


def solution(mesh):
    gx, gy = mesh.shape["gx"], mesh.shape["gy"]

    def local(tensor, sketch_one, sketch_two):
        rows_one, rows_two, depth = tensor.shape
        width = sketch_one.shape[2]
        fits = (
            gx > 1
            and gy % gx == 0
            and depth % gx == 0
            and width % BLOCK == 0
            and rows_two % (8 * gx) == 0
            and rows_one % (8 * gy) == 0
            and width % (8 * gy) == 0
        )
        if fits:
            return local_kernels(gx, gy, tensor, sketch_one, sketch_two)
        return local_plain(tensor, sketch_one, sketch_two)

    in_specs = (P("gx", "gy", None), P("gy", None, None), P("gx", None, None))
    out_specs = (P("gx", None), P("gy", None), P("gx", "gy", None))
    return jax.shard_map(local, mesh=mesh, in_specs=in_specs, out_specs=out_specs, check_vma=False)
```

time: 121 us -> 93.5 us (0.77)
  Pallas kernels: 114 us -> 87.2 us
    pallas_call x5 -> x1, Pallas kernels: 114 us -> 87.2 us  [local_kernels(): pl.pallas_call(functools.partial(kernel, gx, gy), out_shape=[jax.ShapeDty...]
    unnamed x6, local copies, waits for them, and re-layouts: 3.48 us -> 1.75 us
where the time goes in v2:
time: 93.5 us; the launch traced here: 91.6 us
  Pallas kernels  87.2 us (93%)
  local copies, waits for them, and re-layouts  3.78 us (4%)
    pallas_call x1, Pallas kernels, local_kernels(): pl.pallas_call(functools.partial(kernel, gx, gy), out_shape=[jax.ShapeDty...  87.2 us

profile of v2, /device:TPU:0, one launch (start us, length us, event | category | flops | bytes accessed | tf_op | source)
XLA Modules:
  0.0 91.6 jit_solution(3207752402110370637)
XLA Ops:
  0.6 87.2 %shard_map.58 = (f32[256,256]{1,0:T(8,128)}, f32[128,256]{1,0:T(8,128)}, f32[8,2,32,32]{3,2,1,0:T(8,128)}) custom-call(f32[256,8,128]{2,1,0:T(8,128)} %bitcast.6, f32[128,8,256]{2,1,0:T(8,128)} %s1_hbm.1, f32[64,8,256]{2,1,0:T(8,128)} %s2_hbm.1), custom_call_target="tpu_custom_call" | custom-call | tf_op jit(solution)/shard_map/pallas_call | solution.py:394
  87.8 1.2 %copy.6 = f32[2,32,32,4,2]{1,0,4,3,2:T(2,128)S(1)} copy(f32[2,32,32,4,2]{2,1,4,0,3:T(8,128)} %bitcast.7) | data formatting | bytes 131072 | tf_op jit(solution)/shard_map/transpose | solution.py:419
  89.0 0.0 copy-start
  89.0 0.8 reshape.13
  89.8 0.1 copy-done
  89.9 0.0 copy-start.1
  89.9 0.7 copy.9
  90.6 0.3 copy-done.1
  90.9 0.7 copy.10
Async XLA Ops:
  89.0 1.0 %copy-start = (f32[256,256]{1,0:T(8,128)S(1)}, f32[256,256]{1,0:T(8,128)}, u32[]{:S(2)}) copy-start(f32[256,256]{1,0:T(8,128)} %get-tuple-element.12) | copy-start | bytes 786436
  89.9 1.0 %copy-start.1 = (f32[128,256]{1,0:T(8,128)S(1)}, f32[128,256]{1,0:T(8,128)}, u32[]{:S(2)}) copy-start(f32[128,256]{1,0:T(8,128)} %get-tuple-element.13) | copy-start | bytes 393220

commit v3 on v2

--- a/solution.py
+++ b/solution.py
@@ -255,11 +255,17 @@
                 device_id={"gx": b // ratio, "gy": 0},
                 device_id_type=MESH,
             ).wait_recv()
-            out_ref[s] = got[s]
 
         @pl.when(own)
         def _():
-            out_ref[s] = pieces[b]
+            got[s] = pieces[b]
+
+    per = pieces.shape[1]
+    for sa in range(gx):
+        for k in range(per):
+            out_ref[:, sa * per + k, :] = jnp.concatenate(
+                [got[sa * ratio + sb, k] for sb in range(ratio)], axis=1
+            )
 
     for g in range(gy):
         @pl.when(jnp.logical_not(jnp.logical_and(inside, g == b)))
@@ -275,7 +281,7 @@
     zall, zslots, zsend, zrecv,
     s2_all, s2_got, s2send, s2recv,
     spart, sfull, sslots, ssend, srecv,
-    hpart, hfull, hslots, hsend, hrecv,
+    hpart, hfull, hslots, hsend, hrecv, bsend, brecv,
     wall, wslots, wsend, wrecv,
     pieces, got, esend, erecv,
 ):
@@ -359,17 +365,30 @@
     def send_second():
         w_moves.extend(scatter_start(wall, wslots, wsend, wrecv, "gy", gy, lead_chunk))
 
-    reduce_rows(
-        hpart, hfull, hslots, hsend, hrecv, "gy", gy, beside=contract_second, after=send_second
-    )
+    band = width // gx
+    strip = band // gy
+
+    def strip_chunk(ref, index):
+        return ref.at[pl.ds(pl.multiple_of(a * band + index * strip, strip), strip)]
+
+    copies = scatter_start(hpart, hslots, hsend.at[0], hrecv.at[0], "gy", gy, strip_chunk)
+    contract_second()
+    finish(copies)
+    mine = pl.ds(pl.multiple_of(a * band + b * strip, strip), strip)
+    hfull[mine, :] = sum_chunk(hpart, hslots, mine)
+    copies = gather_start(hfull, hsend.at[1], hrecv.at[1], "gy", gy, strip_chunk)
+    send_second()
+    finish(copies)
+    finish(gather_start(hfull, bsend, brecv, "gx", gx, row_chunk(band)))
     factor_inverse(hfull[...], work)
     q2_ref[...] = nt(sfull[...], work[:, width:])
     finish(w_moves)
     w = sum_chunk(wall, wslots, b)
-    for g in range(gy):
-        inv = work[g * part : (g + 1) * part, width:]
-        for k in range(per):
-            pieces[g, k] = nt(w[k], inv)
+    inv = work[:, width : 2 * width]
+    for k in range(per):
+        turned = nt(inv, w[k])
+        for g in range(gy):
+            pieces[g, k] = turned[g * part : (g + 1) * part]
     exchange_pieces(gx, gy, pieces, got, out_ref, esend, erecv)
 
 
@@ -391,12 +410,12 @@
 
     turned = jnp.swapaxes(tensor, 1, 2)
     vmem = pl.BlockSpec(memory_space=pltpu.VMEM)
-    basis_one, basis_two, got = pl.pallas_call(
+    basis_one, basis_two, core = pl.pallas_call(
         functools.partial(kernel, gx, gy),
         out_shape=[
             jax.ShapeDtypeStruct((rows_one, width), f32),
             jax.ShapeDtypeStruct((rows_two, width), f32),
-            jax.ShapeDtypeStruct((gy, per, part, part), f32),
+            jax.ShapeDtypeStruct((part, depth, ranks), f32),
         ],
         in_specs=[pl.BlockSpec(memory_space=pl.ANY)] * 3,
         out_specs=[vmem] * 3,
@@ -408,7 +427,8 @@
             V(gx, per, width, rows_two), V(gx - 1, per, width, rows_two), D(gx - 1), D(gx - 1),
             V(gx, per, ranks, width), V(gx - 1, per, ranks, width), D(gx - 1), D(gx - 1),
             *sums(rows_two, gx),
-            *sums(width, gy),
+            V(width, width), V(width, width), V(gy - 1, width // (gx * gy), width),
+            D(2, gy - 1), D(2, gy - 1), D(gx - 1), D(gx - 1),
             V(gy, per, part, width), V(gy - 1, per, part, width), D(gy - 1), D(gy - 1),
             V(gy, per, part, part), V(gy, per, part, part), D(gy), D(gy),
         ],
@@ -416,8 +436,7 @@
             vmem_limit_bytes=VMEM_BYTES, collective_id=1, has_side_effects=True
         ),
     )(turned, sketch_one, sketch_two)
-    core = got.reshape(gx, gy // gx, per, part, part).transpose(1, 3, 4, 0, 2)
-    return basis_one, basis_two, core.reshape(ranks, part, depth)
+    return basis_one, basis_two, jnp.transpose(core, (2, 0, 1))
 
 
 def solution(mesh):
@@ -433,7 +452,7 @@
             and width % BLOCK == 0
             and rows_two % (8 * gx) == 0
             and rows_one % (8 * gy) == 0
-            and width % (8 * gy) == 0
+            and width % (8 * gy * gx) == 0
         )
         if fits:
             return local_kernels(gx, gy, tensor, sketch_one, sketch_two)

time: 93.5 us -> 90.9 us (0.972)
  Pallas kernels: 87.2 us -> 85.3 us
    pallas_call x1, Pallas kernels: 87.2 us -> 85.3 us  [local_kernels(): pl.pallas_call(functools.partial(kernel, gx, gy), out_shape=[jax.ShapeDty...]
    unnamed x6 -> x7, local copies, waits for them, and re-layouts: 1.75 us -> 3.31 us
    transpose x1 -> x0, local copies, waits for them, and re-layouts: 1.19 us -> none  [local_kernels(): core = got.reshape(gx, gy // gx, per, part, part).transpose(1, 3, 4, 0, 2)]
where the time goes in v3:
time: 90.9 us; the launch traced here: 89.2 us
  Pallas kernels  85.3 us (94%)
  local copies, waits for them, and re-layouts  3.31 us (4%)
    pallas_call x1, Pallas kernels, local_kernels(): pl.pallas_call(functools.partial(kernel, gx, gy), out_shape=[jax.ShapeDty...  85.3 us
    unnamed x7, local copies, waits for them, and re-layouts  3.31 us

profile of v3, /device:TPU:0, one launch (start us, length us, event | category | flops | bytes accessed | tf_op | source)
XLA Modules:
  0.0 89.2 jit_solution(9468448742219598312)
XLA Ops:
  0.6 85.3 %shard_map.58 = (f32[256,256]{1,0:T(8,128)}, f32[128,256]{1,0:T(8,128)}, f32[32,8,64]{2,1,0:T(8,128)}) custom-call(f32[256,8,128]{2,1,0:T(8,128)} %bitcast.2, f32[128,8,256]{2,1,0:T(8,128)} %s1_hbm.1, f32[64,8,256]{2,1,0:T(8,128)} %s2_hbm.1), custom_call_target="tpu_custom_call" | custom-call | tf_op jit(solution)/shard_map/pallas_call | solution.py:413
  85.9 0.0 copy-start.1
  85.9 1.7 %copy.9 = f32[256,256]{1,0:T(8,128)} copy(f32[256,256]{1,0:T(8,128)} %get-tuple-element.12) | data formatting | bytes 524288
  87.6 0.0 copy-done.1
  87.6 0.0 copy-start
  87.6 0.7 copy.10
  88.3 0.3 copy-done
  88.6 0.7 copy.11
Async XLA Ops:
  85.9 1.7 %copy-start.1 = (f32[128,256]{1,0:T(8,128)S(1)}, f32[128,256]{1,0:T(8,128)}, u32[]{:S(2)}) copy-start(f32[128,256]{1,0:T(8,128)} %get-tuple-element.13) | copy-start | bytes 393220
  87.6 1.0 %copy-start = (f32[32,8,64]{2,1,0:T(8,128)S(1)}, f32[32,8,64]{2,1,0:T(8,128)}, u32[]{:S(2)}) copy-start(f32[32,8,64]{2,1,0:T(8,128)} %get-tuple-element.8) | copy-start | bytes 196612

commit v4 on v3

--- a/solution.py
+++ b/solution.py
@@ -221,6 +221,30 @@
     finish(copies)
 
 
+def pair_start(blocks, slots, send, recv, axis):
+    me = lax.axis_index(axis)
+    other = 1 - lax.rem(me, 2)
+    return start_copy(
+        blocks.at[other], slots, send, recv, axis, (me // 2) * 2 + other
+    )
+
+
+def across_start(blocks, slots, middle, target, send, recv, axis, size):
+    me = lax.axis_index(axis)
+    inner, outer = lax.rem(me, 2), me // 2
+    middle[...] = blocks[inner] + slots[...]
+    copies = []
+    for d in range(1, size // 2):
+        peer = lax.rem(outer + d, size // 2)
+        copies.append(
+            start_copy(
+                middle.at[peer], target.at[d - 1], send.at[d - 1], recv.at[d - 1], axis,
+                peer * 2 + inner,
+            )
+        )
+    return copies
+
+
 def exchange_pieces(gx, gy, pieces, got, out_ref, send, recv):
     a, b = lax.axis_index("gx"), lax.axis_index("gy")
     ratio = gy // gx
@@ -278,11 +302,11 @@
     t_ref, s1_ref, s2_ref, load, work,
     ypart, yfull, yslots, ysend, yrecv,
     gpart, gfull, gslots, gsend, grecv,
-    zall, zslots, zsend, zrecv,
+    zall, zpair, zmid, zslots, zsend, zrecv,
     s2_all, s2_got, s2send, s2recv,
     spart, sfull, sslots, ssend, srecv,
     hpart, hfull, hslots, hsend, hrecv, bsend, brecv,
-    wall, wslots, wsend, wrecv,
+    wall, wpair, wmid, wslots, wsend, wrecv,
     pieces, got, esend, erecv,
 ):
     depth = t_ref.shape[1]
@@ -319,19 +343,21 @@
 
     def contract():
         for k in range(depth):
-            zall[k // per, k % per] = nn(yt, t_ref[:, k, :])
+            zall[(k // per) % 2, k // per // 2, k % per] = nn(yt, t_ref[:, k, :])
 
     def send_contraction():
-        z_moves.extend(scatter_start(zall, zslots, zsend, zrecv, "gx", gx, lead_chunk))
+        z_moves.append(pair_start(zall, zpair, zsend.at[gx // 2 - 1], zrecv.at[gx // 2 - 1], "gx"))
 
     reduce_rows(
         gpart, gfull, gslots, gsend, grecv, "gx", gx, beside=contract, after=send_contraction
     )
+    finish(z_moves)
+    z_moves = across_start(zall, zpair, zmid, zslots, zsend, zrecv, "gx", gx)
     factor_inverse(gfull[...], work)
     inv = work[:, width : 2 * width]
     q1_ref[...] = nt(yfull[...], inv)
     finish(z_moves)
-    z = sum_chunk(zall, zslots, a)
+    z = sum_chunk(zmid, zslots, a // 2)
     p = [nn(inv, z[k]) for k in range(per)]
 
     finish(for_later)
@@ -353,17 +379,17 @@
 
     sketch = sfull[...]
     hpart[...] = tn(sketch, sketch)
-    part = wall.shape[2]
+    part = wall.shape[3]
     w_moves = []
 
     def contract_second():
         for k in range(per):
             w = nn(p[k], sketch)
             for g in range(gy):
-                wall[g, k] = w[g * part : (g + 1) * part]
+                wall[g % 2, g // 2, k] = w[g * part : (g + 1) * part]
 
     def send_second():
-        w_moves.extend(scatter_start(wall, wslots, wsend, wrecv, "gy", gy, lead_chunk))
+        w_moves.append(pair_start(wall, wpair, wsend.at[gy // 2 - 1], wrecv.at[gy // 2 - 1], "gy"))
 
     band = width // gx
     strip = band // gy
@@ -380,10 +406,12 @@
     send_second()
     finish(copies)
     finish(gather_start(hfull, bsend, brecv, "gx", gx, row_chunk(band)))
+    finish(w_moves)
+    w_moves = across_start(wall, wpair, wmid, wslots, wsend, wrecv, "gy", gy)
     factor_inverse(hfull[...], work)
     q2_ref[...] = nt(sfull[...], work[:, width:])
     finish(w_moves)
-    w = sum_chunk(wall, wslots, b)
+    w = sum_chunk(wmid, wslots, b // 2)
     inv = work[:, width : 2 * width]
     for k in range(per):
         turned = nt(inv, w[k])
@@ -424,12 +452,16 @@
             V(width, max(2, per) * width),
             *sums(rows_one, gy),
             *sums(width, gx),
-            V(gx, per, width, rows_two), V(gx - 1, per, width, rows_two), D(gx - 1), D(gx - 1),
+            V(2, gx // 2, per, width, rows_two), V(gx // 2, per, width, rows_two),
+            V(gx // 2, per, width, rows_two), V(gx // 2 - 1, per, width, rows_two),
+            D(gx // 2), D(gx // 2),
             V(gx, per, ranks, width), V(gx - 1, per, ranks, width), D(gx - 1), D(gx - 1),
             *sums(rows_two, gx),
             V(width, width), V(width, width), V(gy - 1, width // (gx * gy), width),
             D(2, gy - 1), D(2, gy - 1), D(gx - 1), D(gx - 1),
-            V(gy, per, part, width), V(gy - 1, per, part, width), D(gy - 1), D(gy - 1),
+            V(2, gy // 2, per, part, width), V(gy // 2, per, part, width),
+            V(gy // 2, per, part, width), V(gy // 2 - 1, per, part, width),
+            D(gy // 2), D(gy // 2),
             V(gy, per, part, part), V(gy, per, part, part), D(gy), D(gy),
         ],
         compiler_params=pltpu.CompilerParams(
@@ -446,7 +478,8 @@
         rows_one, rows_two, depth = tensor.shape
         width = sketch_one.shape[2]
         fits = (
-            gx > 1
+            gx > 2
+            and gx % 2 == 0
             and gy % gx == 0
             and depth % gx == 0
             and width % BLOCK == 0

time: 90.9 us -> 86.5 us (0.952)
  Pallas kernels: 85.3 us -> 81.1 us
    pallas_call x1, Pallas kernels: 85.3 us -> 81.1 us  [local_kernels(): pl.pallas_call(functools.partial(kernel, gx, gy), out_shape=[jax.ShapeDty...]
where the time goes in v4:
time: 86.5 us; the launch traced here: 85 us
  Pallas kernels  81.1 us (94%)
  local copies, waits for them, and re-layouts  3.31 us (4%)
    pallas_call x1, Pallas kernels, local_kernels(): pl.pallas_call(functools.partial(kernel, gx, gy), out_shape=[jax.ShapeDty...  81.1 us
    unnamed x7, local copies, waits for them, and re-layouts  3.31 us

profile of v4, /device:TPU:0, one launch (start us, length us, event | category | flops | bytes accessed | tf_op | source)
XLA Modules:
  0.0 85.0 jit_solution(13256711954015552436)
XLA Ops:
  0.6 81.1 %shard_map.58 = (f32[256,256]{1,0:T(8,128)}, f32[128,256]{1,0:T(8,128)}, f32[32,8,64]{2,1,0:T(8,128)}) custom-call(f32[256,8,128]{2,1,0:T(8,128)} %bitcast.2, f32[128,8,256]{2,1,0:T(8,128)} %s1_hbm.1, f32[64,8,256]{2,1,0:T(8,128)} %s2_hbm.1), custom_call_target="tpu_custom_call" | custom-call | tf_op jit(solution)/shard_map/pallas_call | solution.py:441
  81.7 0.0 copy-start.1
  81.7 1.7 %copy.9 = f32[256,256]{1,0:T(8,128)} copy(f32[256,256]{1,0:T(8,128)} %get-tuple-element.12) | data formatting | bytes 524288
  83.4 0.0 copy-done.1
  83.4 0.0 copy-start
  83.4 0.7 copy.10
  84.1 0.3 copy-done
  84.4 0.7 copy.11
Async XLA Ops:
  81.7 1.7 %copy-start.1 = (f32[128,256]{1,0:T(8,128)S(1)}, f32[128,256]{1,0:T(8,128)}, u32[]{:S(2)}) copy-start(f32[128,256]{1,0:T(8,128)} %get-tuple-element.13) | copy-start | bytes 393220
  83.4 1.0 %copy-start = (f32[32,8,64]{2,1,0:T(8,128)S(1)}, f32[32,8,64]{2,1,0:T(8,128)}, u32[]{:S(2)}) copy-start(f32[32,8,64]{2,1,0:T(8,128)} %get-tuple-element.8) | copy-start | bytes 196612
